TPU v7x, 256 devices: a whole 4x4x8 slice. The times are simulated.
256 devices in a mesh: leaf: 16 (over x, y), row: 16 (over z, core).
Axes of the slice: x: 4, y: 4, z: 8, core: 2. Of those that a mesh axis runs over, the one named last changes fastest.
Arguments:
- rhs: bfloat16 [6, 16, 512, 256], P(None, 'leaf', 'row'), may hold values from -6 to 6
- diag_inverse: bfloat16 [16, 6, 512, 512], P('leaf'), as said below
- factor: bfloat16 [16, 178, 512, 512], P('leaf', None, 'row'), as said below
- widths: int32 [6, 16], P(None, 'leaf'), may hold values from 64 to 512, as said below
- structure: int32 [16, 178], P('leaf'), may hold values from 0 to 1, as said below
Outputs:
- forward_solution: bfloat16 [6, 16, 512, 256], P(None, 'leaf', 'row')
- adjoint_solution: bfloat16 [6, 16, 512, 256], P(None, 'leaf', 'row')
Inputs may be any that keep to these rules, and one draw needn't show every extreme that they name: `widths`: every draw has a supernode of exactly 512 columns and one of exactly one eighth of 512 columns. `structure`: 1 where the block is present. Each diag_inverse[j, l] is lower triangular with diagonal entries from 0.5 to 1. `factor`: dense blocks of independent entries.
All inputs are finite; a program needn't handle non-finite values.
Results may differ from a plain program's by a relative error of at most 0.017.
Values may be sent and summed in bfloat16 or wider, within the bound.
A program may use at most 64 MiB of HBM per device.

v0:
```python
import jax
import jax.numpy as jnp
from jax import lax
from jax.sharding import PartitionSpec as P


def group_size(level_now, leaf_count):
    return min(2**level_now, leaf_count)


def block_offsets(levels, leaf_count):
    offset_table = {}
    cursor = 0
    for source_level in range(levels):
        for target_level in range(source_level + 1, levels):
            offset_table[source_level, target_level] = cursor
            cursor += group_size(target_level, leaf_count)
    return offset_table


def blocks_after(level_now, levels, leaf_count):
    return sum(
        (group_size(target_level, leaf_count) for target_level in range(level_now + 1, levels))
    )


def contract_rows(left_side, right_side):
    return lax.dot_general(
        left_side, right_side, (((0,), (0,)), ((), ())), preferred_element_type=jnp.float32
    )


def apply_columns(matrix, shard_piece):
    return jnp.dot(matrix, shard_piece, preferred_element_type=jnp.float32)


def group_reduce(partials, group_span, leaf_count, leaf_index):
    group_base = leaf_index // group_span * group_span
    spread = jnp.zeros((leaf_count,) + partials.shape[1:], jnp.float32)
    spread = lax.dynamic_update_slice_in_dim(spread, partials, group_base, 0)
    return lax.psum_scatter(
        spread.astype(jnp.bfloat16), "leaf", scatter_dimension=0, tiled=True
    ).astype(jnp.float32)[0]


def group_collect(own_block, group_span, leaf_index):
    everyone = lax.all_gather(own_block[None], "leaf", axis=0, tiled=True)
    group_base = leaf_index // group_span * group_span
    return lax.dynamic_slice_in_dim(everyone, group_base, group_span, 0)


def adjoint_level(flat_blocks, flat_values, own_full, full_mask, block_mask, inverse_cols):
    pulled = lax.psum(contract_rows(flat_blocks, flat_values).astype(jnp.bfloat16), "row").astype(
        jnp.float32
    )
    reduced_full = (full_mask[:, None] * (own_full.astype(jnp.float32) - pulled)).astype(
        jnp.bfloat16
    )
    solved = contract_rows(inverse_cols, reduced_full)
    return (block_mask[:, None] * solved).astype(jnp.bfloat16)


def shards(rhs, diag_inverse, factor, widths, structure):
    leaf_count = lax.axis_size("leaf")
    leaf_index = lax.axis_index("leaf")
    row_index = lax.axis_index("row")
    levels = rhs.shape[0]
    block_rows = rhs.shape[2]
    columns = rhs.shape[3]
    full_width = factor.shape[3]
    inverse = diag_inverse[0]
    blocks = factor[0]
    weights = structure[0].astype(jnp.float32)
    own_rows = row_index * block_rows
    positions = jnp.arange(full_width, dtype=jnp.int32)
    full_masks = (positions[None, :] < widths).astype(jnp.float32)
    block_masks = lax.dynamic_slice_in_dim(full_masks, own_rows, block_rows, 1)
    offset_table = block_offsets(levels, leaf_count)
    pending = {}
    for target_level in range(1, levels):
        pending[target_level] = jnp.zeros(
            (group_size(target_level, leaf_count), block_rows, columns), jnp.float32
        )
    forward_blocks = []
    forward_full = []
    for level_now in range(levels):
        if level_now > 0:
            incoming = group_reduce(
                pending[level_now], group_size(level_now, leaf_count), leaf_count, leaf_index
            )
        else:
            incoming = jnp.zeros((block_rows, columns), jnp.float32)
        residual = (
            block_masks[level_now][:, None] * (rhs[level_now, 0].astype(jnp.float32) - incoming)
        ).astype(jnp.bfloat16)
        solve_rows = inverse[level_now]
        folded = apply_columns(solve_rows, lax.all_gather(residual, "row", axis=0, tiled=True))
        solved_full = (full_masks[level_now][:, None] * folded).astype(jnp.bfloat16)
        solved_block = lax.dynamic_slice_in_dim(solved_full, own_rows, block_rows, 0)
        forward_blocks.append(solved_block)
        forward_full.append(solved_full)
        if level_now + 1 < levels:
            first_block = offset_table[level_now, level_now + 1]
            block_count = blocks_after(level_now, levels, leaf_count)
            chosen = blocks[first_block : first_block + block_count].reshape(
                block_count * block_rows, full_width
            )
            products = jnp.dot(chosen, solved_full, preferred_element_type=jnp.float32).reshape(
                block_count, block_rows, columns
            )
            products = products * weights[first_block : first_block + block_count][:, None, None]
            cursor = 0
            for target_level in range(level_now + 1, levels):
                group_span = group_size(target_level, leaf_count)
                pending[target_level] = (
                    pending[target_level] + products[cursor : cursor + group_span]
                )
                cursor += group_span
    gathered = {}
    adjoint_blocks = [None] * levels
    for level_now in reversed(range(levels)):
        inverse_cols = lax.dynamic_slice_in_dim(inverse[level_now], own_rows, block_rows, 1)
        if level_now + 1 == levels:
            solved = contract_rows(inverse_cols, forward_full[level_now])
            own_adjoint = (block_masks[level_now][:, None] * solved).astype(jnp.bfloat16)
        else:
            first_block = offset_table[level_now, level_now + 1]
            block_count = blocks_after(level_now, levels, leaf_count)
            stacked = jnp.concatenate(
                [gathered[upper_level] for upper_level in range(level_now + 1, levels)], 0
            )
            stacked = stacked * structure[0, first_block : first_block + block_count][
                :, None, None
            ].astype(jnp.bfloat16)
            flat_blocks = blocks[first_block : first_block + block_count].reshape(
                block_count * block_rows, full_width
            )
            flat_values = stacked.reshape(block_count * block_rows, columns)
            own_adjoint = adjoint_level(
                flat_blocks,
                flat_values,
                forward_full[level_now],
                full_masks[level_now],
                block_masks[level_now],
                inverse_cols,
            )
        adjoint_blocks[level_now] = own_adjoint
        if level_now > 0:
            gathered[level_now] = group_collect(
                own_adjoint, group_size(level_now, leaf_count), leaf_index
            )
    return (jnp.stack(forward_blocks)[:, None], jnp.stack(adjoint_blocks)[:, None])


def solution(mesh):
    placed = (
        P(None, "leaf", "row", None),
        P("leaf", None, None, None),
        P("leaf", None, "row", None),
        P(None, "leaf"),
        P("leaf", None),
    )
    return jax.shard_map(
        shards,
        mesh=mesh,
        in_specs=placed,
        out_specs=(P(None, "leaf", "row", None), P(None, "leaf", "row", None)),
        check_vma=False,
    )
```

profile of v0, /device:TPU:1, one launch (start us, length us, event | category | flops | bytes accessed | tf_op | source)
XLA Modules:
  0.0 1223.9 jit_solution(11152830773635222627)
XLA Ops:
  8.9 22.0 %all_gather.33 = bf16[512,256]{1,0:T(8,128)(2,1)S(1)} all-gather(bf16[32,256]{1,0:T(8,128)(2,1)S(1)} %fusion.72), channel_id=1, replica_groups=mesh['leaf'=16,'row'=16] {'row'}, dimensions={0}, use_global_device_ids=true | all-gather | bytes 278528 | tf_op jit(solution)/shard_map/all_gather | solution.py:97
  30.9 1.6 slice.219
  32.6 1.4 fusion
  36.8 1.5 slice.228
  38.4 71.6 %reduce-scatter.16.cloned.1.call-done = bf16[1,32,256]{2,1,0:T(8,128)(2,1)} async-done(((bf16[16,32,256]{2,1,0:T(8,128)(2,1)}), bf16[1,32,256]{2,1,0:T(8,128)(2,1)}) %reduce-scatter.16.cloned.1.call-update) | async-done | bytes 16400
  110.8 20.2 %all_gather.34 = bf16[512,256]{1,0:T(8,128)(2,1)S(1)} all-gather(bf16[32,256]{1,0:T(8,128)(2,1)S(1)} %fusion.71), channel_id=1, replica_groups=mesh['leaf'=16,'row'=16] {'row'}, dimensions={0}, use_global_device_ids=true | all-gather | bytes 278528 | tf_op jit(solution)/shard_map/all_gather | solution.py:97
  131.0 1.4 fusion.1
  133.1 1.7 convolution_bitcast_fusion.1
  134.8 2.9 copy.19
  137.7 1.5 broadcast_multiply_fusion.1
  142.1 2.5 slice.238
  144.7 69.2 %reduce-scatter.18.cloned.1.call-done = bf16[1,32,256]{2,1,0:T(8,128)(2,1)} async-done(((bf16[16,32,256]{2,1,0:T(8,128)(2,1)}), bf16[1,32,256]{2,1,0:T(8,128)(2,1)}) %reduce-scatter.18.cloned.1.call-update) | async-done | bytes 16400
  214.8 20.3 %all_gather.35 = bf16[512,256]{1,0:T(8,128)(2,1)S(1)} all-gather(bf16[32,256]{1,0:T(8,128)(2,1)S(1)} %fusion.69), channel_id=1, replica_groups=mesh['leaf'=16,'row'=16] {'row'}, dimensions={0}, use_global_device_ids=true | all-gather | bytes 278528 | tf_op jit(solution)/shard_map/all_gather | solution.py:97
  235.1 1.4 fusion.2
  237.2 1.6 convolution_bitcast_fusion
  238.8 2.8 copy.20
  241.6 1.5 broadcast_multiply_fusion.2
  246.0 2.3 slice.249
  248.5 69.3 %reduce-scatter.20.cloned.1.call-done = bf16[1,32,256]{2,1,0:T(8,128)(2,1)} async-done(((bf16[16,32,256]{2,1,0:T(8,128)(2,1)}), bf16[1,32,256]{2,1,0:T(8,128)(2,1)}) %reduce-scatter.20.cloned.1.call-update) | async-done | bytes 16400
  318.6 20.2 %all_gather.36 = bf16[512,256]{1,0:T(8,128)(2,1)S(1)} all-gather(bf16[32,256]{1,0:T(8,128)(2,1)S(1)} %fusion.67), channel_id=1, replica_groups=mesh['leaf'=16,'row'=16] {'row'}, dimensions={0}, use_global_device_ids=true | all-gather | bytes 278528 | tf_op jit(solution)/shard_map/all_gather | solution.py:97
  338.9 1.4 fusion.3
  341.0 1.5 convolution_bitcast_fusion.2
  342.5 2.6 copy.21
  347.5 2.2 fusion.21
  352.1 69.4 %reduce-scatter.22.cloned.1.call-done = bf16[1,32,256]{2,1,0:T(8,128)(2,1)} async-done(((bf16[16,32,256]{2,1,0:T(8,128)(2,1)}), bf16[1,32,256]{2,1,0:T(8,128)(2,1)}) %reduce-scatter.22.cloned.1.call-update) | async-done | bytes 16400
  422.3 20.3 %all_gather.37 = bf16[512,256]{1,0:T(8,128)(2,1)S(1)} all-gather(bf16[32,256]{1,0:T(8,128)(2,1)S(1)} %fusion.65), channel_id=1, replica_groups=mesh['leaf'=16,'row'=16] {'row'}, dimensions={0}, use_global_device_ids=true | all-gather | bytes 278528 | tf_op jit(solution)/shard_map/all_gather | solution.py:97
  442.6 1.4 fusion.4
  445.9 2.1 copy.22
  448.0 2.5 fusion.20
  451.1 3.5 fusion.86
  454.7 67.7 %reduce-scatter.24.cloned.1.call-done = bf16[1,32,256]{2,1,0:T(8,128)(2,1)} async-done(((bf16[16,32,256]{2,1,0:T(8,128)(2,1)}), bf16[1,32,256]{2,1,0:T(8,128)(2,1)}) %reduce-scatter.24.cloned.1.call-update) | async-done | bytes 16400
  523.2 20.2 %all_gather.38 = bf16[512,256]{1,0:T(8,128)(2,1)S(1)} all-gather(bf16[32,256]{1,0:T(8,128)(2,1)S(1)} %fusion.63), channel_id=1, replica_groups=mesh['leaf'=16,'row'=16] {'row'}, dimensions={0}, use_global_device_ids=true | all-gather | bytes 278528 | tf_op jit(solution)/shard_map/all_gather | solution.py:97
  543.4 1.4 fusion.5
  546.1 18.0 %all-gather = bf16[512,256]{1,0:T(8,128)(2,1)S(1)} all-gather(bf16[32,256]{1,0:T(8,128)(2,1)S(1)} %fusion.11), channel_id=2, replica_groups=mesh['leaf'=16,'row'=16] {'leaf'}, dimensions={0}, use_global_device_ids=true | all-gather | bytes 278528 | tf_op jit(solution)/shard_map/all_gather | solution.py:47
  565.9 1.6 dynamic-slice_bitcast_fusion.4
  567.5 1.5 copy.23
  569.0 105.7 %all-reduce.11.cloned.1.call-done = bf16[512,256]{0,1:T(8,128)(2,1)} async-done(((bf16[512,256]{0,1:T(8,128)(2,1)}), bf16[512,256]{0,1:T(8,128)(2,1)}) %all-reduce.11.cloned.1.call-update) | async-done | bytes 262160 | tf_op jit(solution)/shard_map/psum | solution.py:53
  676.1 18.5 %all-gather.1 = bf16[512,256]{1,0:T(8,128)(2,1)S(1)} all-gather(bf16[32,256]{1,0:T(8,128)(2,1)S(1)} %fusion.12), channel_id=3, replica_groups=mesh['leaf'=16,'row'=16] {'leaf'}, dimensions={0}, use_global_device_ids=true | all-gather | bytes 278528 | tf_op jit(solution)/shard_map/all_gather | solution.py:47
  699.9 109.0 %all-reduce.13.cloned.1.call-done = bf16[512,256]{0,1:T(8,128)(2,1)} async-done(((bf16[512,256]{0,1:T(8,128)(2,1)}), bf16[512,256]{0,1:T(8,128)(2,1)}) %all-reduce.13.cloned.1.call-update) | async-done | bytes 262160 | tf_op jit(solution)/shard_map/psum | solution.py:53
  808.9 1.5 fusion.13
  810.4 18.5 %all-gather.2 = bf16[512,256]{1,0:T(8,128)(2,1)S(1)} all-gather(bf16[32,256]{1,0:T(8,128)(2,1)S(1)} %fusion.13), channel_id=4, replica_groups=mesh['leaf'=16,'row'=16] {'leaf'}, dimensions={0}, use_global_device_ids=true | all-gather | bytes 278528 | tf_op jit(solution)/shard_map/all_gather | solution.py:47
  832.3 1.6 dynamic-slice_bitcast_fusion.2
  833.9 1.5 copy.25
  837.5 107.2 %all-reduce.15.cloned.1.call-done = bf16[512,256]{0,1:T(8,128)(2,1)} async-done(((bf16[512,256]{0,1:T(8,128)(2,1)}), bf16[512,256]{0,1:T(8,128)(2,1)}) %all-reduce.15.cloned.1.call-update) | async-done | bytes 262160 | tf_op jit(solution)/shard_map/psum | solution.py:53
  946.1 18.7 %all-gather.3 = bf16[512,256]{1,0:T(8,128)(2,1)S(1)} all-gather(bf16[32,256]{1,0:T(8,128)(2,1)S(1)} %fusion.14), channel_id=5, replica_groups=mesh['leaf'=16,'row'=16] {'leaf'}, dimensions={0}, use_global_device_ids=true | all-gather | bytes 278528 | tf_op jit(solution)/shard_map/all_gather | solution.py:47
  969.6 110.7 %all-reduce.17.cloned.1.call-done = bf16[512,256]{0,1:T(8,128)(2,1)} async-done(((bf16[512,256]{0,1:T(8,128)(2,1)}), bf16[512,256]{0,1:T(8,128)(2,1)}) %all-reduce.17.cloned.1.call-update) | async-done | bytes 262160 | tf_op jit(solution)/shard_map/psum | solution.py:53
  1081.7 18.5 %all-gather.4 = bf16[512,256]{1,0:T(8,128)(2,1)S(1)} all-gather(bf16[32,256]{1,0:T(8,128)(2,1)S(1)} %fusion.15), channel_id=6, replica_groups=mesh['leaf'=16,'row'=16] {'leaf'}, dimensions={0}, use_global_device_ids=true | all-gather | bytes 278528 | tf_op jit(solution)/shard_map/all_gather | solution.py:47
  1103.9 111.1 %all-reduce.19.cloned.1.call-done = bf16[512,256]{0,1:T(8,128)(2,1)} async-done(((bf16[512,256]{0,1:T(8,128)(2,1)}), bf16[512,256]{0,1:T(8,128)(2,1)}) %all-reduce.19.cloned.1.call-update) | async-done | bytes 262160 | tf_op jit(solution)/shard_map/psum | solution.py:53
  (186 shorter events, 52.1 us)
Async XLA Ops:
  7.2 102.8 %reduce-scatter.16.cloned.1.call-start = ((), (), s32[]{:S(2)}) async-start(), calls=%async_computation.10 | async-start | bytes 278528
  8.0 24.6 %copy-start.31 = (f32[1,512]{1,0:T(1,128)}, f32[1,512]{1,0:T(1,128)S(1)}, u32[]{:S(2)}) copy-start(f32[1,512]{1,0:T(1,128)S(1)} %get-tuple-element.19) | copy-start | bytes 6148
  8.0 123.0 %copy-start.33 = (f32[1,512]{1,0:T(1,128)}, f32[1,512]{1,0:T(1,128)S(1)}, u32[]{:S(2)}) copy-start(f32[1,512]{1,0:T(1,128)S(1)} %get-tuple-element.18) | copy-start | bytes 6148
  8.0 227.1 %copy-start.35 = (f32[1,512]{1,0:T(1,128)}, f32[1,512]{1,0:T(1,128)S(1)}, u32[]{:S(2)}) copy-start(f32[1,512]{1,0:T(1,128)S(1)} %get-tuple-element.17) | copy-start | bytes 6148
  8.0 330.9 %copy-start.36 = (f32[1,512]{1,0:T(1,128)}, f32[1,512]{1,0:T(1,128)S(1)}, u32[]{:S(2)}) copy-start(f32[1,512]{1,0:T(1,128)S(1)} %get-tuple-element.16) | copy-start | bytes 6148
  8.0 434.6 %copy-start.37 = (f32[1,512]{1,0:T(1,128)}, f32[1,512]{1,0:T(1,128)S(1)}, u32[]{:S(2)}) copy-start(f32[1,512]{1,0:T(1,128)S(1)} %get-tuple-element.15) | copy-start | bytes 6148
  8.1 0.8 copy-start.38
  8.1 101.9 %copy-start.40 = (f32[32]{0:T(128)}, f32[32]{0:T(128)S(1)}, u32[]{:S(2)}) copy-start(f32[32]{0:T(128)S(1)} %get-tuple-element.24) | copy-start | bytes 388
  8.1 205.8 %copy-start.42 = (f32[32]{0:T(128)}, f32[32]{0:T(128)S(1)}, u32[]{:S(2)}) copy-start(f32[32]{0:T(128)S(1)} %get-tuple-element.23) | copy-start | bytes 388
  8.1 309.6 %copy-start.43 = (f32[32]{0:T(128)}, f32[32]{0:T(128)S(1)}, u32[]{:S(2)}) copy-start(f32[32]{0:T(128)S(1)} %get-tuple-element.22) | copy-start | bytes 388
  8.1 413.4 %copy-start.44 = (f32[32]{0:T(128)}, f32[32]{0:T(128)S(1)}, u32[]{:S(2)}) copy-start(f32[32]{0:T(128)S(1)} %get-tuple-element.21) | copy-start | bytes 388
  30.9 1.6 copy-start.46
  34.8 1.2 copy-start
  36.7 73.2 %copy-start.29 = (bf16[6,1,32,256]{3,2,1,0:T(8,128)(2,1)S(1)}, bf16[6,1,32,256]{3,2,1,0:T(8,128)(2,1)}, u32[]{:S(2)}) copy-start(bf16[6,1,32,256]{3,2,1,0:T(8,128)(2,1)} %param.5) | copy-start | bytes 294916
  36.7 177.2 %reduce-scatter.18.cloned.1.call-start = ((), (), s32[]{:S(2)}) async-start(), calls=%async_computation.11 | async-start | bytes 278528
  139.3 1.1 copy-start.1
  142.0 175.7 %reduce-scatter.20.cloned.1.call-start = ((), (), s32[]{:S(2)}) async-start(), calls=%async_computation.12 | async-start | bytes 278528
  213.9 23.3 %copy-start.2 = (bf16[1,40,32,512]{3,2,1,0:T(8,128)(2,1)S(1)}, bf16[1,40,32,512]{3,2,1,0:T(8,128)(2,1)}, u32[]{:S(2)}) copy-start(bf16[1,40,32,512]{3,2,1,0:T(8,128)(2,1)} %slice.238) | copy-start | bytes 3932164
  243.1 1.1 copy-start.4
  245.9 175.6 %reduce-scatter.22.cloned.1.call-start = ((), (), s32[]{:S(2)}) async-start(), calls=%async_computation.13 | async-start | bytes 278528
  317.7 23.2 %copy-start.7 = (bf16[1,32,32,512]{3,2,1,0:T(8,128)(2,1)S(1)}, bf16[1,32,32,512]{3,2,1,0:T(8,128)(2,1)}, u32[]{:S(2)}) copy-start(bf16[1,32,32,512]{3,2,1,0:T(8,128)(2,1)} %slice.249) | copy-start | bytes 3145732
  346.4 1.0 copy-start.9
  349.7 172.6 %reduce-scatter.24.cloned.1.call-start = ((), (), s32[]{:S(2)}) async-start(), calls=%async_computation.14 | async-start | bytes 278528
  350.9 95.0 %copy-start.5 = (bf16[1,16,32,512]{3,2,1,0:T(8,128)(2,1)}, bf16[1,16,32,512]{3,2,1,0:T(8,128)(2,1)S(1)}, u32[]{:S(2)}) copy-start(bf16[1,16,32,512]{3,2,1,0:T(8,128)(2,1)S(1)} %slice.261) | copy-start | bytes 1572868
  444.0 0.7 copy-start.13
  450.5 224.2 %all-reduce.11.cloned.1.call-start = ((), (), s32[]{:S(2)}) async-start(), calls=%async_computation.5 | async-start | bytes 524288 | tf_op jit(solution)/shard_map/psum | solution.py:53
  522.3 41.9 %copy-start.6 = (bf16[1,16,32,512]{3,2,1,0:T(8,128)(2,1)S(1)}, bf16[1,16,32,512]{3,2,1,0:T(8,128)(2,1)}, u32[]{:S(2)}) copy-start(bf16[1,16,32,512]{3,2,1,0:T(8,128)(2,1)} %copy-done.5) | copy-start | bytes 1572868
  544.8 19.2 %copy-start.24 = (bf16[256,512]{1,0:T(8,128)(2,1)}, bf16[256,512]{1,0:T(8,128)(2,1)S(1)}, u32[]{:S(2)}) copy-start(bf16[256,512]{1,0:T(8,128)(2,1)S(1)} %fusion.5) | copy-start | bytes 786436
  544.8 129.9 %copy-start.14 = (bf16[256,512]{1,0:T(8,128)(2,1)S(1)}, bf16[256,512]{1,0:T(8,128)(2,1)}, u32[]{:S(2)}) copy-start(bf16[256,512]{1,0:T(8,128)(2,1)} %copy-done.13) | copy-start | bytes 786436
  565.2 243.7 %all-reduce.13.cloned.1.call-start = ((), (), s32[]{:S(2)}) async-start(), calls=%async_computation.6 | async-start | bytes 524288 | tf_op jit(solution)/shard_map/psum | solution.py:53
  674.7 20.6 %copy-start.8 = (bf16[1,32,32,512]{3,2,1,0:T(8,128)(2,1)S(1)}, bf16[1,32,32,512]{3,2,1,0:T(8,128)(2,1)}, u32[]{:S(2)}) copy-start(bf16[1,32,32,512]{3,2,1,0:T(8,128)(2,1)} %slice.249) | copy-start | bytes 3145732
  676.1 18.5 %copy-start.25 = (bf16[32,256]{1,0:T(8,128)(2,1)}, bf16[32,256]{1,0:T(8,128)(2,1)S(1)}, u32[]{:S(2)}) copy-start(bf16[32,256]{1,0:T(8,128)(2,1)S(1)} %fusion.12) | copy-start | bytes 49156
  696.5 248.2 %all-reduce.15.cloned.1.call-start = ((), (), s32[]{:S(2)}) async-start(), calls=%async_computation.7 | async-start | bytes 524288 | tf_op jit(solution)/shard_map/psum | solution.py:53
  808.9 22.1 %copy-start.3 = (bf16[1,40,32,512]{3,2,1,0:T(8,128)(2,1)S(1)}, bf16[1,40,32,512]{3,2,1,0:T(8,128)(2,1)}, u32[]{:S(2)}) copy-start(bf16[1,40,32,512]{3,2,1,0:T(8,128)(2,1)} %slice.238) | copy-start | bytes 3932164
  810.4 21.8 %copy-start.27 = (bf16[32,256]{1,0:T(8,128)(2,1)}, bf16[32,256]{1,0:T(8,128)(2,1)S(1)}, u32[]{:S(2)}) copy-start(bf16[32,256]{1,0:T(8,128)(2,1)S(1)} %fusion.13) | copy-start | bytes 49156
  832.3 248.0 %all-reduce.17.cloned.1.call-start = ((), (), s32[]{:S(2)}) async-start(), calls=%async_computation.8 | async-start | bytes 524288 | tf_op jit(solution)/shard_map/psum | solution.py:53
  964.8 0.7 copy-start.23
  966.5 1.4 copy-start.30
  966.5 113.7 %copy-start.34 = (f32[1,512]{1,0:T(1,128)S(1)}, f32[1,512]{1,0:T(1,128)}, u32[]{:S(2)}) copy-start(f32[1,512]{1,0:T(1,128)} %copy-done.33) | copy-start | bytes 6148
  966.5 113.7 %copy-start.41 = (f32[32]{0:T(128)S(1)}, f32[32]{0:T(128)}, u32[]{:S(2)}) copy-start(f32[32]{0:T(128)} %copy-done.40) | copy-start | bytes 388
  967.8 133.2 %copy-start.19 = (bf16[512,256]{1,0:T(8,128)(2,1)S(1)}, bf16[512,256]{1,0:T(8,128)(2,1)}, u32[]{:S(2)}) copy-start(bf16[512,256]{1,0:T(8,128)(2,1)} %copy-done.18) | copy-start | bytes 786436
  967.9 133.2 %copy-start.47 = (bf16[46]{0:T(256)(128)(2,1)S(1)}, bf16[46]{0:T(256)(128)(2,1)}, u32[]{:S(2)}) copy-start(bf16[46]{0:T(256)(128)(2,1)} %slice_bitcast_fusion) | copy-start | bytes 280
  967.9 247.1 %all-reduce.19.cloned.1.call-start = ((), (), s32[]{:S(2)}) async-start(), calls=%async_computation.9 | async-start | bytes 524288 | tf_op jit(solution)/shard_map/psum | solution.py:53
  1101.2 113.8 %copy-start.11 = (bf16[256,512]{1,0:T(8,128)(2,1)S(1)}, bf16[256,512]{1,0:T(8,128)(2,1)}, u32[]{:S(2)}) copy-start(bf16[256,512]{1,0:T(8,128)(2,1)} %copy-done.10) | copy-start | bytes 786436
  1101.2 113.8 %copy-start.32 = (f32[1,512]{1,0:T(1,128)S(1)}, f32[1,512]{1,0:T(1,128)}, u32[]{:S(2)}) copy-start(f32[1,512]{1,0:T(1,128)} %copy-done.31) | copy-start | bytes 6148
  1101.3 113.8 %copy-start.39 = (f32[32]{0:T(128)S(1)}, f32[32]{0:T(128)}, u32[]{:S(2)}) copy-start(f32[32]{0:T(128)} %copy-done.38) | copy-start | bytes 388
  1101.3 115.1 %copy-start.28 = (bf16[32,256]{1,0:T(8,128)(2,1)S(1)}, bf16[32,256]{1,0:T(8,128)(2,1)}, u32[]{:S(2)}) copy-start(bf16[32,256]{1,0:T(8,128)(2,1)} %copy-done.27) | copy-start | bytes 49156
  1101.3 115.1 %copy-start.26 = (bf16[32,256]{1,0:T(8,128)(2,1)S(1)}, bf16[32,256]{1,0:T(8,128)(2,1)}, u32[]{:S(2)}) copy-start(bf16[32,256]{1,0:T(8,128)(2,1)} %copy-done.25) | copy-start | bytes 49156
  (10 other events, 6.9 us)
Sparse Core Ops, SparseCore 0:
  36.8 73.0 reduce-scatter.15
  142.2 71.6 reduce-scatter.17
  246.1 71.6 reduce-scatter.19
  349.8 71.6 reduce-scatter.21
  450.6 71.6 reduce-scatter.23
  565.4 109.3 all-reduce.10
  696.6 112.2 all-reduce.12
  832.4 112.2 all-reduce.14
  968.0 112.2 all-reduce.16
  1102.7 112.2 all-reduce.18
where the time goes:
time: 1230 us; the launch traced here: 1220 us
  waiting for transfers between devices  891 us (72%)
  blocking collectives  215 us (17%)
  local copies, waits for them, and re-layouts  53.4 us (4%)
  matrix products  29 us (2%)
  other arithmetic  19.6 us (2%)
  between operations  15 us (1%)
    psum x5, waiting for transfers between devices, adjoint_level(): lax.psum(contract_rows(flat_blocks, flat_values).astype(jnp.bfloat16), 'r...  544 us
    unnamed x15, waiting for transfers between devices  347 us
    all_gather x6, blocking collectives, shards(): lax.all_gather(residual, 'row', axis=0, tiled=True)  123 us
    all_gather x5, blocking collectives, group_collect(): everyone = lax.all_gather(own_block[None], 'leaf', axis=0, tiled=True)  92.2 us
  transfers between devices with their start and end apart: 10, of which 10 were waited for; matrix products, arithmetic and copies ran while one was open for 2% of the time, Pallas kernels for 0%

commit v1 on v0

--- a/solution.py
+++ b/solution.py
@@ -94,7 +94,12 @@
             block_masks[level_now][:, None] * (rhs[level_now, 0].astype(jnp.float32) - incoming)
         ).astype(jnp.bfloat16)
         solve_rows = inverse[level_now]
-        folded = apply_columns(solve_rows, lax.all_gather(residual, "row", axis=0, tiled=True))
+        folded = apply_columns(
+            solve_rows,
+            jnp.concatenate(
+                lax.all_to_all(jnp.stack([residual] * lax.axis_size("row")), "row", 0, 0), axis=0
+            ),
+        )
         solved_full = (full_masks[level_now][:, None] * folded).astype(jnp.bfloat16)
         solved_block = lax.dynamic_slice_in_dim(solved_full, own_rows, block_rows, 0)
         forward_blocks.append(solved_block)

time: 1230 us -> 1220 us (level)
  blocking collectives: 215 us -> 91.9 us
  waiting for transfers between devices: 891 us -> 949 us
  starting transfers between devices: 0.41 us -> 57.1 us
    all_gather x6 -> x0, blocking collectives: 123 us -> none  [shards(): lax.all_gather(residual, 'row', axis=0, tiled=True)]
    all_to_all x0 -> x6, starting transfers between devices: none -> 56.5 us  [shards(): lax.all_to_all(jnp.stack([residual] * lax.axis_size('row')), 'row', 0, 0)]
    all_to_all x0 -> x6, waiting for transfers between devices: none -> 55.7 us  [shards(): lax.all_to_all(jnp.stack([residual] * lax.axis_size('row')), 'row', 0, 0)]
  transfers between devices with their start and end apart: 10 -> 16, of which waited for: 10 -> 16; matrix products, arithmetic and copies ran while one was open for 2% -> 3% of each run, Pallas kernels for 0% -> 0%
where the time goes in v1:
time: 1220 us
  waiting for transfers between devices  949 us (78%)
  blocking collectives  91.9 us (8%)
  local copies, waits for them, and re-layouts  57.7 us (5%)
  starting transfers between devices  57.1 us (5%)
  matrix products  30.6 us (3%)
  other arithmetic  20.1 us (2%)
  between operations  15 us (1%)
    psum x5, waiting for transfers between devices, adjoint_level(): lax.psum(contract_rows(flat_blocks, flat_values).astype(jnp.bfloat16), 'r...  542 us
    unnamed x15, waiting for transfers between devices  352 us
    all_gather x5, blocking collectives, group_collect(): everyone = lax.all_gather(own_block[None], 'leaf', axis=0, tiled=True)  91.9 us
    all_to_all x6, starting transfers between devices, shards(): lax.all_to_all(jnp.stack([residual] * lax.axis_size('row')), 'row', 0, 0)  56.5 us
    all_to_all x6, waiting for transfers between devices, shards(): lax.all_to_all(jnp.stack([residual] * lax.axis_size('row')), 'row', 0, 0)  55.7 us
  transfers between devices with their start and end apart: 16, of which 16 were waited for; matrix products, arithmetic and copies ran while one was open for 3% of the time, Pallas kernels for 0%

profile of v1, /device:TPU:1, one launch (start us, length us, event | category | flops | bytes accessed | tf_op | source)
XLA Modules:
  0.0 1221.8 jit_solution(7019565486835438566)
XLA Ops:
  9.6 10.0 all-to-all-start
  20.3 1.5 slice.230
  22.0 9.3 all-to-all-done
  35.4 72.3 %reduce-scatter.16.cloned.1.call-done = bf16[1,32,256]{2,1,0:T(8,128)(2,1)} async-done(((bf16[16,32,256]{2,1,0:T(8,128)(2,1)}), bf16[1,32,256]{2,1,0:T(8,128)(2,1)}) %reduce-scatter.16.cloned.1.call-update) | async-done | bytes 16400
  109.2 9.3 all-to-all-start.1
  118.5 1.5 slice.240
  120.2 10.1 all-to-all-done.1
  132.3 1.7 convolution_bitcast_fusion.1
  134.0 2.9 copy.19
  136.9 1.5 broadcast_multiply_fusion.1
  141.2 70.3 %reduce-scatter.18.cloned.1.call-done = bf16[1,32,256]{2,1,0:T(8,128)(2,1)} async-done(((bf16[16,32,256]{2,1,0:T(8,128)(2,1)}), bf16[1,32,256]{2,1,0:T(8,128)(2,1)}) %reduce-scatter.18.cloned.1.call-update) | async-done | bytes 16400
  213.0 9.3 all-to-all-start.2
  222.3 2.5 slice.251
  224.9 9.1 all-to-all-done.2
  236.1 3.0 convolution_bitcast_fusion
  239.0 2.8 copy.20
  246.2 70.0 %reduce-scatter.20.cloned.1.call-done = bf16[1,32,256]{2,1,0:T(8,128)(2,1)} async-done(((bf16[16,32,256]{2,1,0:T(8,128)(2,1)}), bf16[1,32,256]{2,1,0:T(8,128)(2,1)}) %reduce-scatter.20.cloned.1.call-update) | async-done | bytes 16400
  317.7 9.3 all-to-all-start.3
  327.1 2.3 slice.263
  329.5 9.3 all-to-all-done.3
  338.8 1.5 fusion.3
  340.9 1.5 convolution_bitcast_fusion.2
  342.5 2.6 copy.21
  347.5 2.2 fusion.21
  349.8 70.1 %reduce-scatter.22.cloned.1.call-done = bf16[1,32,256]{2,1,0:T(8,128)(2,1)} async-done(((bf16[16,32,256]{2,1,0:T(8,128)(2,1)}), bf16[1,32,256]{2,1,0:T(8,128)(2,1)}) %reduce-scatter.22.cloned.1.call-update) | async-done | bytes 16400
  421.3 9.3 all-to-all-start.4
  431.9 10.6 all-to-all-done.4
  445.8 2.1 copy.22
  447.8 2.5 fusion.20
  451.6 69.0 %reduce-scatter.24.cloned.1.call-done = bf16[1,32,256]{2,1,0:T(8,128)(2,1)} async-done(((bf16[16,32,256]{2,1,0:T(8,128)(2,1)}), bf16[1,32,256]{2,1,0:T(8,128)(2,1)}) %reduce-scatter.24.cloned.1.call-update) | async-done | bytes 16400
  522.1 9.3 all-to-all-start.5
  532.1 3.6 fusion.91
  535.6 7.5 all-to-all-done.5
  545.8 17.8 %all-gather = bf16[512,256]{1,0:T(8,128)(2,1)S(1)} all-gather(bf16[32,256]{1,0:T(8,128)(2,1)S(1)} %fusion.11), channel_id=2, replica_groups=mesh['leaf'=16,'row'=16] {'leaf'}, dimensions={0}, use_global_device_ids=true | all-gather | bytes 278528 | tf_op jit(solution)/shard_map/all_gather | solution.py:47
  565.5 1.6 dynamic-slice_bitcast_fusion.4
  567.1 1.5 copy.23
  568.6 104.0 %all-reduce.11.cloned.1.call-done = bf16[512,256]{0,1:T(8,128)(2,1)} async-done(((bf16[512,256]{0,1:T(8,128)(2,1)}), bf16[512,256]{0,1:T(8,128)(2,1)}) %all-reduce.11.cloned.1.call-update) | async-done | bytes 262160 | tf_op jit(solution)/shard_map/psum | solution.py:53
  674.0 18.5 %all-gather.1 = bf16[512,256]{1,0:T(8,128)(2,1)S(1)} all-gather(bf16[32,256]{1,0:T(8,128)(2,1)S(1)} %fusion.12), channel_id=3, replica_groups=mesh['leaf'=16,'row'=16] {'leaf'}, dimensions={0}, use_global_device_ids=true | all-gather | bytes 278528 | tf_op jit(solution)/shard_map/all_gather | solution.py:47
  697.8 109.0 %all-reduce.13.cloned.1.call-done = bf16[512,256]{0,1:T(8,128)(2,1)} async-done(((bf16[512,256]{0,1:T(8,128)(2,1)}), bf16[512,256]{0,1:T(8,128)(2,1)}) %all-reduce.13.cloned.1.call-update) | async-done | bytes 262160 | tf_op jit(solution)/shard_map/psum | solution.py:53
  806.9 1.5 fusion.13
  808.4 18.5 %all-gather.2 = bf16[512,256]{1,0:T(8,128)(2,1)S(1)} all-gather(bf16[32,256]{1,0:T(8,128)(2,1)S(1)} %fusion.13), channel_id=4, replica_groups=mesh['leaf'=16,'row'=16] {'leaf'}, dimensions={0}, use_global_device_ids=true | all-gather | bytes 278528 | tf_op jit(solution)/shard_map/all_gather | solution.py:47
  830.5 1.6 dynamic-slice_bitcast_fusion.2
  832.1 1.5 copy.25
  835.7 107.0 %all-reduce.15.cloned.1.call-done = bf16[512,256]{0,1:T(8,128)(2,1)} async-done(((bf16[512,256]{0,1:T(8,128)(2,1)}), bf16[512,256]{0,1:T(8,128)(2,1)}) %all-reduce.15.cloned.1.call-update) | async-done | bytes 262160 | tf_op jit(solution)/shard_map/psum | solution.py:53
  944.1 18.5 %all-gather.3 = bf16[512,256]{1,0:T(8,128)(2,1)S(1)} all-gather(bf16[32,256]{1,0:T(8,128)(2,1)S(1)} %fusion.14), channel_id=5, replica_groups=mesh['leaf'=16,'row'=16] {'leaf'}, dimensions={0}, use_global_device_ids=true | all-gather | bytes 278528 | tf_op jit(solution)/shard_map/all_gather | solution.py:47
  967.4 110.7 %all-reduce.17.cloned.1.call-done = bf16[512,256]{0,1:T(8,128)(2,1)} async-done(((bf16[512,256]{0,1:T(8,128)(2,1)}), bf16[512,256]{0,1:T(8,128)(2,1)}) %all-reduce.17.cloned.1.call-update) | async-done | bytes 262160 | tf_op jit(solution)/shard_map/psum | solution.py:53
  1079.5 18.5 %all-gather.4 = bf16[512,256]{1,0:T(8,128)(2,1)S(1)} all-gather(bf16[32,256]{1,0:T(8,128)(2,1)S(1)} %fusion.15), channel_id=6, replica_groups=mesh['leaf'=16,'row'=16] {'leaf'}, dimensions={0}, use_global_device_ids=true | all-gather | bytes 278528 | tf_op jit(solution)/shard_map/all_gather | solution.py:47
  1101.8 111.1 %all-reduce.19.cloned.1.call-done = bf16[512,256]{0,1:T(8,128)(2,1)} async-done(((bf16[512,256]{0,1:T(8,128)(2,1)}), bf16[512,256]{0,1:T(8,128)(2,1)}) %all-reduce.19.cloned.1.call-update) | async-done | bytes 262160 | tf_op jit(solution)/shard_map/psum | solution.py:53
  (194 shorter events, 65.7 us)
Async XLA Ops:
  8.0 13.9 %copy-start.37 = (f32[32]{0:T(128)}, f32[32]{0:T(128)S(1)}, u32[]{:S(2)}) copy-start(f32[32]{0:T(128)S(1)} %get-tuple-element.25) | copy-start | bytes 388
  8.0 99.7 %copy-start.39 = (f32[32]{0:T(128)}, f32[32]{0:T(128)S(1)}, u32[]{:S(2)}) copy-start(f32[32]{0:T(128)S(1)} %get-tuple-element.24) | copy-start | bytes 388
  8.0 203.5 %copy-start.41 = (f32[32]{0:T(128)}, f32[32]{0:T(128)S(1)}, u32[]{:S(2)}) copy-start(f32[32]{0:T(128)S(1)} %get-tuple-element.23) | copy-start | bytes 388
  8.0 308.2 %copy-start.42 = (f32[32]{0:T(128)}, f32[32]{0:T(128)S(1)}, u32[]{:S(2)}) copy-start(f32[32]{0:T(128)S(1)} %get-tuple-element.22) | copy-start | bytes 388
  8.0 411.8 %copy-start.43 = (f32[32]{0:T(128)}, f32[32]{0:T(128)S(1)}, u32[]{:S(2)}) copy-start(f32[32]{0:T(128)S(1)} %get-tuple-element.21) | copy-start | bytes 388
  9.6 21.7 %all-to-all-start = ((bf16[16,32,256]{2,1,0:T(8,128)(2,1)}), bf16[16,32,256]{2,1,0:T(8,128)(2,1)S(1)}, u32[]{:S(2)}, u32[]{:S(2)}) async-start(bf16[16,32,256]{2,1,0:T(8,128)(2,1)} %stack.40), calls=%async_computation | async-start | bytes 524288 | tf_op jit(solution)/shard_map/all_to_all | solution.py:100
  19.5 88.1 %reduce-scatter.16.cloned.1.call-start = ((), (), s32[]{:S(2)}) async-start(), calls=%async_computation.16 | async-start | bytes 278528
  21.9 11.3 copy-start.30
  21.9 108.3 %copy-start.32 = (f32[1,512]{1,0:T(1,128)}, f32[1,512]{1,0:T(1,128)S(1)}, u32[]{:S(2)}) copy-start(f32[1,512]{1,0:T(1,128)S(1)} %get-tuple-element.18) | copy-start | bytes 6148
  22.0 212.0 %copy-start.34 = (f32[1,512]{1,0:T(1,128)}, f32[1,512]{1,0:T(1,128)S(1)}, u32[]{:S(2)}) copy-start(f32[1,512]{1,0:T(1,128)S(1)} %get-tuple-element.17) | copy-start | bytes 6148
  22.0 316.8 %copy-start.35 = (f32[1,512]{1,0:T(1,128)}, f32[1,512]{1,0:T(1,128)S(1)}, u32[]{:S(2)}) copy-start(f32[1,512]{1,0:T(1,128)S(1)} %get-tuple-element.16) | copy-start | bytes 6148
  22.0 420.5 %copy-start.36 = (f32[1,512]{1,0:T(1,128)}, f32[1,512]{1,0:T(1,128)S(1)}, u32[]{:S(2)}) copy-start(f32[1,512]{1,0:T(1,128)S(1)} %get-tuple-element.15) | copy-start | bytes 6148
  33.3 74.3 %copy-start.28 = (bf16[6,1,32,256]{3,2,1,0:T(8,128)(2,1)S(1)}, bf16[6,1,32,256]{3,2,1,0:T(8,128)(2,1)}, u32[]{:S(2)}) copy-start(bf16[6,1,32,256]{3,2,1,0:T(8,128)(2,1)} %param.5) | copy-start | bytes 294916
  33.5 1.2 copy-start
  109.2 21.0 %all-to-all-start.1 = ((bf16[16,32,256]{2,1,0:T(8,128)(2,1)}), bf16[16,32,256]{2,1,0:T(8,128)(2,1)S(1)}, u32[]{:S(2)}, u32[]{:S(2)}) async-start(bf16[16,32,256]{2,1,0:T(8,128)(2,1)} %stack.43), calls=%async_computation.1 | async-start | bytes 524288 | tf_op jit(solution)/shard_map/all_to_all | solution.py:100
  118.5 92.9 %reduce-scatter.18.cloned.1.call-start = ((), (), s32[]{:S(2)}) async-start(), calls=%async_computation.17 | async-start | bytes 278528
  213.0 21.0 %all-to-all-start.2 = ((bf16[16,32,256]{2,1,0:T(8,128)(2,1)}), bf16[16,32,256]{2,1,0:T(8,128)(2,1)S(1)}, u32[]{:S(2)}, u32[]{:S(2)}) async-start(bf16[16,32,256]{2,1,0:T(8,128)(2,1)} %stack.46), calls=%async_computation.2 | async-start | bytes 524288 | tf_op jit(solution)/shard_map/all_to_all | solution.py:100
  222.3 94.0 %reduce-scatter.20.cloned.1.call-start = ((), (), s32[]{:S(2)}) async-start(), calls=%async_computation.18 | async-start | bytes 278528
  243.3 1.1 copy-start.3
  317.7 21.0 %all-to-all-start.3 = ((bf16[16,32,256]{2,1,0:T(8,128)(2,1)}), bf16[16,32,256]{2,1,0:T(8,128)(2,1)S(1)}, u32[]{:S(2)}, u32[]{:S(2)}) async-start(bf16[16,32,256]{2,1,0:T(8,128)(2,1)} %stack.49), calls=%async_computation.3 | async-start | bytes 524288 | tf_op jit(solution)/shard_map/all_to_all | solution.py:100
  327.0 92.8 %reduce-scatter.22.cloned.1.call-start = ((), (), s32[]{:S(2)}) async-start(), calls=%async_computation.19 | async-start | bytes 278528
  338.7 2.2 copy-start.6
  421.3 21.1 %all-to-all-start.4 = ((bf16[16,32,256]{2,1,0:T(8,128)(2,1)}), bf16[16,32,256]{2,1,0:T(8,128)(2,1)}, u32[]{:S(2)}, u32[]{:S(2)}) async-start(bf16[16,32,256]{2,1,0:T(8,128)(2,1)} %stack.52), calls=%async_computation.4 | async-start | bytes 524288 | tf_op jit(solution)/shard_map/all_to_all | solution.py:100
  430.6 89.9 %reduce-scatter.24.cloned.1.call-start = ((), (), s32[]{:S(2)}) async-start(), calls=%async_computation.20 | async-start | bytes 278528
  431.8 16.1 %copy-start.4 = (bf16[1,16,32,512]{3,2,1,0:T(8,128)(2,1)}, bf16[1,16,32,512]{3,2,1,0:T(8,128)(2,1)S(1)}, u32[]{:S(2)}) copy-start(bf16[1,16,32,512]{3,2,1,0:T(8,128)(2,1)S(1)} %slice.276) | copy-start | bytes 1572868
  522.1 21.0 %all-to-all-start.5 = ((bf16[16,32,256]{2,1,0:T(8,128)(2,1)}), bf16[16,32,256]{2,1,0:T(8,128)(2,1)S(1)}, u32[]{:S(2)}, u32[]{:S(2)}) async-start(bf16[16,32,256]{2,1,0:T(8,128)(2,1)} %stack.55), calls=%async_computation.5 | async-start | bytes 524288 | tf_op jit(solution)/shard_map/all_to_all | solution.py:100
  531.4 141.2 %all-reduce.11.cloned.1.call-start = ((), (), s32[]{:S(2)}) async-start(), calls=%async_computation.11 | async-start | bytes 524288 | tf_op jit(solution)/shard_map/psum | solution.py:53
  543.1 20.7 %copy-start.5 = (bf16[1,16,32,512]{3,2,1,0:T(8,128)(2,1)S(1)}, bf16[1,16,32,512]{3,2,1,0:T(8,128)(2,1)}, u32[]{:S(2)}) copy-start(bf16[1,16,32,512]{3,2,1,0:T(8,128)(2,1)} %copy-done.4) | copy-start | bytes 1572868
  544.6 19.1 %copy-start.23 = (bf16[256,512]{1,0:T(8,128)(2,1)}, bf16[256,512]{1,0:T(8,128)(2,1)S(1)}, u32[]{:S(2)}) copy-start(bf16[256,512]{1,0:T(8,128)(2,1)S(1)} %fusion.5) | copy-start | bytes 786436
  544.6 128.1 %copy-start.13 = (bf16[256,512]{1,0:T(8,128)(2,1)S(1)}, bf16[256,512]{1,0:T(8,128)(2,1)}, u32[]{:S(2)}) copy-start(bf16[256,512]{1,0:T(8,128)(2,1)} %copy-done.12) | copy-start | bytes 786436
  564.9 242.0 %all-reduce.13.cloned.1.call-start = ((), (), s32[]{:S(2)}) async-start(), calls=%async_computation.12 | async-start | bytes 524288 | tf_op jit(solution)/shard_map/psum | solution.py:53
  672.6 20.6 %copy-start.7 = (bf16[1,32,32,512]{3,2,1,0:T(8,128)(2,1)S(1)}, bf16[1,32,32,512]{3,2,1,0:T(8,128)(2,1)}, u32[]{:S(2)}) copy-start(bf16[1,32,32,512]{3,2,1,0:T(8,128)(2,1)} %slice.263) | copy-start | bytes 3145732
  674.0 18.5 %copy-start.24 = (bf16[32,256]{1,0:T(8,128)(2,1)}, bf16[32,256]{1,0:T(8,128)(2,1)S(1)}, u32[]{:S(2)}) copy-start(bf16[32,256]{1,0:T(8,128)(2,1)S(1)} %fusion.12) | copy-start | bytes 49156
  694.4 248.3 %all-reduce.15.cloned.1.call-start = ((), (), s32[]{:S(2)}) async-start(), calls=%async_computation.13 | async-start | bytes 524288 | tf_op jit(solution)/shard_map/psum | solution.py:53
  806.9 22.1 %copy-start.2 = (bf16[1,40,32,512]{3,2,1,0:T(8,128)(2,1)S(1)}, bf16[1,40,32,512]{3,2,1,0:T(8,128)(2,1)}, u32[]{:S(2)}) copy-start(bf16[1,40,32,512]{3,2,1,0:T(8,128)(2,1)} %slice.251) | copy-start | bytes 3932164
  808.3 21.9 %copy-start.26 = (bf16[32,256]{1,0:T(8,128)(2,1)}, bf16[32,256]{1,0:T(8,128)(2,1)S(1)}, u32[]{:S(2)}) copy-start(bf16[32,256]{1,0:T(8,128)(2,1)S(1)} %fusion.13) | copy-start | bytes 49156
  830.3 247.8 %all-reduce.17.cloned.1.call-start = ((), (), s32[]{:S(2)}) async-start(), calls=%async_computation.14 | async-start | bytes 524288 | tf_op jit(solution)/shard_map/psum | solution.py:53
  964.4 1.4 copy-start.29
  964.4 113.8 %copy-start.33 = (f32[1,512]{1,0:T(1,128)S(1)}, f32[1,512]{1,0:T(1,128)}, u32[]{:S(2)}) copy-start(f32[1,512]{1,0:T(1,128)} %copy-done.32) | copy-start | bytes 6148
  964.4 113.8 %copy-start.40 = (f32[32]{0:T(128)S(1)}, f32[32]{0:T(128)}, u32[]{:S(2)}) copy-start(f32[32]{0:T(128)} %copy-done.39) | copy-start | bytes 388
  965.7 133.2 %copy-start.18 = (bf16[512,256]{1,0:T(8,128)(2,1)S(1)}, bf16[512,256]{1,0:T(8,128)(2,1)}, u32[]{:S(2)}) copy-start(bf16[512,256]{1,0:T(8,128)(2,1)} %copy-done.17) | copy-start | bytes 786436
  965.7 133.3 %copy-start.45 = (bf16[46]{0:T(256)(128)(2,1)S(1)}, bf16[46]{0:T(256)(128)(2,1)}, u32[]{:S(2)}) copy-start(bf16[46]{0:T(256)(128)(2,1)} %slice_bitcast_fusion) | copy-start | bytes 280
  965.7 247.2 %all-reduce.19.cloned.1.call-start = ((), (), s32[]{:S(2)}) async-start(), calls=%async_computation.15 | async-start | bytes 524288 | tf_op jit(solution)/shard_map/psum | solution.py:53
  1099.1 113.8 %copy-start.10 = (bf16[256,512]{1,0:T(8,128)(2,1)S(1)}, bf16[256,512]{1,0:T(8,128)(2,1)}, u32[]{:S(2)}) copy-start(bf16[256,512]{1,0:T(8,128)(2,1)} %copy-done.9) | copy-start | bytes 786436
  1099.1 113.8 %copy-start.31 = (f32[1,512]{1,0:T(1,128)S(1)}, f32[1,512]{1,0:T(1,128)}, u32[]{:S(2)}) copy-start(f32[1,512]{1,0:T(1,128)} %copy-done.30) | copy-start | bytes 6148
  1099.1 113.8 %copy-start.38 = (f32[32]{0:T(128)S(1)}, f32[32]{0:T(128)}, u32[]{:S(2)}) copy-start(f32[32]{0:T(128)} %copy-done.37) | copy-start | bytes 388
  1099.1 115.1 %copy-start.27 = (bf16[32,256]{1,0:T(8,128)(2,1)S(1)}, bf16[32,256]{1,0:T(8,128)(2,1)}, u32[]{:S(2)}) copy-start(bf16[32,256]{1,0:T(8,128)(2,1)} %copy-done.26) | copy-start | bytes 49156
  1099.1 115.1 %copy-start.25 = (bf16[32,256]{1,0:T(8,128)(2,1)S(1)}, bf16[32,256]{1,0:T(8,128)(2,1)}, u32[]{:S(2)}) copy-start(bf16[32,256]{1,0:T(8,128)(2,1)} %copy-done.24) | copy-start | bytes 49156
  (14 other events, 10.5 us)
Sparse Core Ops, SparseCore 0:
  35.5 72.1 reduce-scatter.15
  141.3 70.0 reduce-scatter.17
  246.3 69.8 reduce-scatter.19
  349.9 69.9 reduce-scatter.21
  450.5 70.0 reduce-scatter.23
  565.0 107.6 all-reduce.10
  694.6 112.2 all-reduce.12
  830.4 112.2 all-reduce.14
  965.8 112.2 all-reduce.16
  1100.6 112.2 all-reduce.18
